TPU v7x, 512 devices: a whole 4x8x8 slice. The times are simulated.
512 devices in a mesh: seq: 64 (over y, z), mp: 8 (over x, core).
Axes of the slice: x: 4, y: 8, z: 8, core: 2. Of those that a mesh axis runs over, the one named last changes fastest.
Arguments:
- inputs: bfloat16 [40960, 6144], P('seq', 'mp'), may hold values from -6 to 6
- queries: bfloat16 [40960, 4096], P('seq', 'mp'), may hold values from -12 to 12
- key_rows: bfloat16 [40960, 4096], P('seq', 'mp'), may hold values from -12 to 12
- values: bfloat16 [40960, 4096], P('seq', 'mp'), may hold values from -6 to 6
- norm_gain: float32 [4096], P('mp'), may hold values from 0.1 to 1.9
- cotangent: bfloat16 [40960, 4096], P('seq', 'mp'), may hold values from -6 to 6
- adapter_down: float32 [32, 6144], P(None, 'mp'), may hold values from -6 to 6
- adapter_up: float32 [32, 4096], P(None, 'mp'), may hold values from -6 to 6
- moment_down: float32 [32, 6144], P(None, 'mp'), may hold values from -6 to 6
- moment_up: float32 [32, 4096], P(None, 'mp'), may hold values from -6 to 6
- noise_down: float32 [32, 6144], P(None, 'mp'), may hold values from -6 to 6
- noise_up: float32 [32, 4096], P(None, 'mp'), may hold values from -6 to 6
Outputs:
- normed: bfloat16 [40960, 4096], P('seq', 'mp')
- new_down: float32 [32, 6144], P(None, 'mp')
- new_moment_down: float32 [32, 6144], P(None, 'mp')
- new_up: float32 [32, 4096], P(None, 'mp')
- new_moment_up: float32 [32, 4096], P(None, 'mp')
All inputs are finite; a program needn't handle non-finite values.
Results may differ from a plain program's by a relative error of at most 0.007.
Values sent between devices are 32-bit elements; how exact they have to be, the bound alone decides.
A program may use at most 128 MiB of HBM per device.

v0:
```python
import math

import jax
import jax.numpy as jnp
from jax import lax
from jax.sharding import PartitionSpec as P

D = 6144
HEAD = 128
RANK = 32
STEP = 250
CYCLE = 1000


friction = 0.2
peak_rate = 0.03
epsilon = 1e-06


def carried_in(x, axis, combine, identity, reverse):
    size, mine = (lax.axis_size(axis), lax.axis_index(axis))
    everything = lax.all_gather(x, axis)
    start = jnp.broadcast_to(jnp.asarray(identity, x.dtype), x.shape)

    def step(k, before):
        at = size - 1 - k if reverse else k
        reached = at > mine if reverse else at < mine
        new = combine(before, everything[at])
        return jnp.where(reached, new, before)

    return lax.fori_loop(0, size, step, start)


def combine_states(earlier, later_part):
    return earlier + later_part


def feature_map(array):
    return (jax.nn.elu(array.astype(jnp.float32)) + 1.0).astype(jnp.bfloat16)


def sghmc_step(parameter, moment, gradient, noise_term):
    step_rate = peak_rate * (math.cos(math.pi * ((STEP - 1) % CYCLE) / CYCLE) + 1.0)
    spread = math.sqrt(2.0 * friction * step_rate)
    moment_new = (1.0 - friction) * moment - step_rate * gradient + spread * noise_term
    return (parameter + moment_new, moment_new)


def per_device(
    inputs,
    queries,
    key_rows,
    values,
    norm_gain,
    cotangent,
    adapter_down,
    adapter_up,
    moment_down,
    moment_up,
    noise_down,
    noise_up,
):
    token_count = queries.shape[0]
    column_count = queries.shape[1]
    heads_here = column_count // HEAD
    blocked = (token_count, heads_here, HEAD)
    down_half = adapter_down.astype(jnp.bfloat16)
    up_half = adapter_up.astype(jnp.bfloat16)
    partial_inner = lax.dot_general(
        down_half, inputs, (((1,), (1,)), ((), ())), preferred_element_type=jnp.float32
    )
    inner_sum = lax.psum(partial_inner, "mp") / math.sqrt(D)
    inner_half = inner_sum.astype(jnp.bfloat16)
    lifted = lax.dot_general(
        inner_half, up_half, (((0,), (0,)), ((), ())), preferred_element_type=jnp.float32
    )
    value_mix = (
        (values.astype(jnp.float32) + lifted / math.sqrt(RANK))
        .astype(jnp.bfloat16)
        .reshape(blocked)
    )
    query_feat = feature_map(queries).reshape(blocked)
    key_feat = feature_map(key_rows).reshape(blocked)
    own_states = jnp.einsum("thd,the->hde", key_feat, value_mix, preferred_element_type=jnp.float32)
    prefix = carried_in(own_states, "seq", combine_states, jnp.zeros_like(own_states), False)
    positions = jnp.arange(token_count, dtype=jnp.int32)
    causal = positions[:, None] >= positions[None, :]
    scores = jnp.einsum("thd,shd->hts", query_feat, key_feat, preferred_element_type=jnp.float32)
    weights = jnp.where(causal[None], scores, 0.0).astype(jnp.bfloat16)
    nearby = jnp.einsum("hts,she->the", weights, value_mix, preferred_element_type=jnp.float32)
    carried = jnp.einsum(
        "thd,hde->the", query_feat, prefix.astype(jnp.bfloat16), preferred_element_type=jnp.float32
    )
    summed = nearby + carried
    gain_rows = norm_gain.reshape(heads_here, HEAD)
    inverse_norm = lax.rsqrt(jnp.mean(summed * summed, axis=-1, keepdims=True) + epsilon)
    unit_rows = summed * inverse_norm
    normed = (gain_rows * unit_rows).astype(jnp.bfloat16).reshape(token_count, column_count)
    gain_grad = gain_rows * cotangent.astype(jnp.float32).reshape(blocked)
    projected = jnp.mean(gain_grad * unit_rows, axis=-1, keepdims=True)
    out_grad = (inverse_norm * (gain_grad - unit_rows * projected)).astype(jnp.bfloat16)
    back_states = jnp.einsum(
        "thd,the->hde", query_feat, out_grad, preferred_element_type=jnp.float32
    )
    suffix = carried_in(back_states, "seq", combine_states, jnp.zeros_like(back_states), True)
    grad_near = jnp.einsum("hts,the->she", weights, out_grad, preferred_element_type=jnp.float32)
    grad_far = jnp.einsum(
        "shd,hde->she", key_feat, suffix.astype(jnp.bfloat16), preferred_element_type=jnp.float32
    )
    grad_half = (grad_near + grad_far).astype(jnp.bfloat16).reshape(token_count, column_count)
    partial_grad = lax.dot_general(
        up_half, grad_half, (((1,), (1,)), ((), ())), preferred_element_type=jnp.float32
    )
    inner_grad = lax.psum(partial_grad, "mp") / math.sqrt(RANK)
    inner_grad_half = inner_grad.astype(jnp.bfloat16)
    grad_down = jnp.dot(inner_grad_half, inputs, preferred_element_type=jnp.float32) / math.sqrt(D)
    grad_up = jnp.dot(inner_half, grad_half, preferred_element_type=jnp.float32) / math.sqrt(RANK)
    down_total, up_total = lax.psum((grad_down, grad_up), "seq")
    new_down, new_moment_down = sghmc_step(adapter_down, moment_down, down_total, noise_down)
    new_up, new_moment_up = sghmc_step(adapter_up, moment_up, up_total, noise_up)
    return (normed, new_down, new_moment_down, new_up, new_moment_up)


def solution(mesh):
    return jax.shard_map(
        per_device,
        mesh=mesh,
        in_specs=(
            P("seq", "mp"),
            P("seq", "mp"),
            P("seq", "mp"),
            P("seq", "mp"),
            P("mp"),
            P("seq", "mp"),
            P(None, "mp"),
            P(None, "mp"),
            P(None, "mp"),
            P(None, "mp"),
            P(None, "mp"),
            P(None, "mp"),
        ),
        out_specs=(P("seq", "mp"), P(None, "mp"), P(None, "mp"), P(None, "mp"), P(None, "mp")),
        check_vma=False,
    )
```

profile of v0, /device:TPU:2, one launch (start us, length us, event | category | flops | bytes accessed | tf_op | source)
XLA Modules:
  0.0 741.7 jit_solution(5236267360927953539)
XLA Ops:
  7.2 1.1 copy-done
  8.4 1.9 fusion.21
  10.7 69.7 %all-reduce.5.cloned.1.call-done = f32[32,640]{1,0:T(8,128)} async-done(((f32[32,640]{1,0:T(8,128)}), f32[32,640]{1,0:T(8,128)}) %all-reduce.5.cloned.1.call-update) | async-done | bytes 81936 | tf_op jit(solution)/shard_map/psum | solution.py:72
  80.4 1.3 fusion.2
  82.6 1.5 fusion.11
  85.0 1.6 copy.37
  86.8 2.9 select_convert_fusion
  89.6 1.7 copy-done.1
  91.3 2.2 fusion.30
  93.5 132.1 %all-gather.5.cloned.1.call-done = f32[256,128,128]{2,1,0:T(8,128)} async-done(((f32[4,128,128]{2,1,0:T(8,128)}), f32[256,128,128]{2,1,0:T(8,128)}) %all-gather.5.cloned.1.call-update) | async-done | bytes 16777232 | tf_op jit(solution)/shard_map/all_gather | solution.py:22
  225.6 68.1 %while.30 = (s32[]{:T(128)}, f32[4,128,128]{2,1,0:T(8,128)S(1)}, s32[]{:T(128)}, f32[64,4,128,128]{3,2,1,0:T(8,128)}, s32[]{:T(128)}, /*index=5*/s32[]{:T(128)}) while((s32[]{:T(128)}, f32[4,128,128]{2,1,0:T(8,128)S(1)}, s32[]{:T(128)}, f32[64,4,128,128]{3,2,1,0:T(8,128)}, s32[]{:T(128)}, /*index=5*/s32[]{:T(128)}) %tuple.95), condition=%wide.region_2.3_spmd.clone, body=%wide.region_1.2_spmd.clone.sunk | while | flops 196612 | bytes 786533 | solution.py:31
  227.7 1.0 add_select_fusion.4
  229.8 1.0 add_select_fusion.4
  232.0 1.0 add_select_fusion.4
  234.1 1.0 add_select_fusion.4
  236.2 1.0 add_select_fusion.4
  238.4 1.0 add_select_fusion.4
  247.9 1.0 add_select_fusion.4
  250.1 1.0 add_select_fusion.4
  252.2 1.0 add_select_fusion.4
  254.3 1.0 add_select_fusion.4
  256.4 1.0 add_select_fusion.4
  258.6 1.0 add_select_fusion.4
  268.2 1.0 add_select_fusion.4
  270.3 1.0 add_select_fusion.4
  272.4 1.0 add_select_fusion.4
  274.5 1.0 add_select_fusion.4
  276.7 1.0 add_select_fusion.4
  278.8 1.0 add_select_fusion.4
  288.4 1.0 add_select_fusion.4
  290.5 1.0 add_select_fusion.4
  292.6 1.0 add_select_fusion.4
  293.7 1.7 multiply_reduce_fusion.1
  295.8 1.2 multiply_convert_fusion
  297.0 1.1 fusion.32
  298.2 3.8 fusion.31
  302.0 134.4 %all-gather.7.cloned.1.call-done = f32[256,128,128]{2,1,0:T(8,128)} async-done(((f32[4,128,128]{2,1,0:T(8,128)}), f32[256,128,128]{2,1,0:T(8,128)}) %all-gather.7.cloned.1.call-update) | async-done | bytes 16777232 | tf_op jit(solution)/shard_map/all_gather | solution.py:22
  436.4 68.5 %while.31 = (s32[]{:T(128)}, f32[4,128,128]{2,1,0:T(8,128)S(1)}, s32[]{:T(128)}, f32[64,4,128,128]{3,2,1,0:T(8,128)}, s32[]{:T(128)}, /*index=5*/s32[]{:T(128)}, s32[]{:T(128)}, s32[]{:T(128)}) while((s32[]{:T(128)}, f32[4,128,128]{2,1,0:T(8,128)S(1)}, s32[]{:T(128)}, f32[64,4,128,128]{3,2,1,0:T(8,128)}, s32[]{:T(128)}, ...), condition=%wide.region_6.7_spmd.clone, body=%wide.region_5.6_spmd.clone.sunk | while | flops 196616 | bytes 786595 | solution.py:31
  436.4 1.1 add_select_fusion.5
  438.6 1.0 add_select_fusion.5
  504.9 2.1 fusion.3
  507.0 1.1 convolution_bitcast_fusion
  509.1 66.0 %all-reduce.7.cloned.1.call-done = f32[32,640]{0,1:T(8,128)} async-done(((f32[32,640]{0,1:T(8,128)}), f32[32,640]{0,1:T(8,128)}) %all-reduce.7.cloned.1.call-update) | async-done | bytes 81936 | tf_op jit(solution)/shard_map/psum | solution.py:114
  575.1 1.9 convolution_multiply_fusion.1
  577.1 1.1 copy.42
  578.2 153.8 %all-reduce.9.cloned.1.call-done = (f32[32,768]{1,0:T(8,128)}, f32[32,512]{1,0:T(8,128)}) async-done(((f32[32,768]{1,0:T(8,128)}, f32[32,512]{1,0:T(8,128)}), (f32[32,768]{1,0:T(8,128)}, f32[32,512]{1,0:T(8,128)})) %all-reduce.9.cloned.1.call-update) | async-done | bytes 163856 | tf_op jit(solution)/shard_map/psum | solution.py:118
  732.0 1.6 fusion.29
  733.6 1.5 fusion.28
  (161 shorter events, 113.0 us)
Async XLA Ops:
  7.2 1.2 copy-start
  7.2 3.2 copy-start.7
  7.2 73.3 %copy-start.9 = (f32[32,512]{1,0:T(8,128)S(1)}, f32[32,512]{1,0:T(8,128)}, u32[]{:S(2)}) copy-start(f32[32,512]{1,0:T(8,128)} %param.23) | copy-start | bytes 196612
  7.2 73.2 %all-reduce.5.cloned.1.call-start = ((), (), s32[]{:S(2)}) async-start(), calls=%async_computation | async-start | bytes 163840 | tf_op jit(solution)/shard_map/psum | solution.py:72
  10.3 72.2 %copy-start.17 = (bf16[640,512]{1,0:T(8,128)(2,1)S(1)}, bf16[640,512]{1,0:T(8,128)(2,1)}, u32[]{:S(2)}) copy-start(bf16[640,512]{1,0:T(8,128)(2,1)} %param.18) | copy-start | bytes 1966084
  10.4 215.2 %all-gather.5.cloned.1.call-start = ((), (), s32[]{:S(2)}) async-start(), calls=%async_computation.2 | async-start | bytes 17039360 | tf_op jit(solution)/shard_map/all_gather | solution.py:22
  81.7 0.8 copy-start.4
  82.5 1.6 copy-start.8
  84.1 352.3 %all-gather.7.cloned.1.call-start = ((), (), s32[]{:S(2)}) async-start(), calls=%async_computation.3 | async-start | bytes 17039360 | tf_op jit(solution)/shard_map/all_gather | solution.py:22
  85.0 208.6 %copy-start.2 = (bf16[640,512]{0,1:T(8,128)(2,1)}, bf16[640,512]{0,1:T(8,128)(2,1)S(1)}, u32[]{:S(2)}) copy-start(bf16[640,512]{0,1:T(8,128)(2,1)S(1)} %copy.47) | copy-start | bytes 1966084
  86.8 4.6 copy-start.5
  89.6 1.7 copy-start.1
  293.7 1.8 copy-start.16
  295.8 1.2 copy-start.3
  298.1 277.0 %all-reduce.7.cloned.1.call-start = ((), (), s32[]{:S(2)}) async-start(), calls=%async_computation.1 | async-start | bytes 655360 | tf_op jit(solution)/shard_map/psum | solution.py:114
  436.4 68.5 %copy-start.18 = (bf16[640,512]{1,0:T(8,128)(2,1)S(1)}, bf16[640,512]{1,0:T(8,128)(2,1)}, u32[]{:S(2)}) copy-start(bf16[640,512]{1,0:T(8,128)(2,1)} %param.18) | copy-start | bytes 1966084
  507.0 1.2 copy-start.11
  508.1 69.0 %copy-start.6 = (bf16[640,4,128]{0,2,1:T(8,128)(2,1)S(1)}, bf16[640,4,128]{0,2,1:T(8,128)(2,1)}, u32[]{:S(2)}) copy-start(bf16[640,4,128]{0,2,1:T(8,128)(2,1)} %get-tuple-element.259) | copy-start | bytes 1966084
  508.1 223.9 %all-reduce.9.cloned.1.call-start = ((), (), s32[]{:S(2)}) async-start(), calls=%async_computation.4 | async-start | bytes 327680 | tf_op jit(solution)/shard_map/psum | solution.py:118
  509.1 222.9 %copy-start.10 = (f32[32,768]{1,0:T(8,128)S(1)}, f32[32,768]{1,0:T(8,128)}, u32[]{:S(2)}) copy-start(f32[32,768]{1,0:T(8,128)} %param.22) | copy-start | bytes 294916
  509.1 222.9 %copy-start.12 = (f32[32,768]{1,0:T(8,128)S(1)}, f32[32,768]{1,0:T(8,128)}, u32[]{:S(2)}) copy-start(f32[32,768]{1,0:T(8,128)} %param.26) | copy-start | bytes 294916
  509.1 222.9 %copy-start.13 = (f32[32,768]{1,0:T(8,128)S(1)}, f32[32,768]{1,0:T(8,128)}, u32[]{:S(2)}) copy-start(f32[32,768]{1,0:T(8,128)} %param.24) | copy-start | bytes 294916
  577.1 156.6 %copy-start.14 = (f32[32,512]{1,0:T(8,128)S(1)}, f32[32,512]{1,0:T(8,128)}, u32[]{:S(2)}) copy-start(f32[32,512]{1,0:T(8,128)} %param.27) | copy-start | bytes 196612
  577.1 156.6 %copy-start.15 = (f32[32,512]{1,0:T(8,128)S(1)}, f32[32,512]{1,0:T(8,128)}, u32[]{:S(2)}) copy-start(f32[32,512]{1,0:T(8,128)} %param.25) | copy-start | bytes 196612
Sparse Core Ops, SparseCore 0:
  10.9 69.4 all-reduce.4
  84.2 141.3 all-gather.4
  298.3 138.1 all-gather.6
  508.3 66.8 all-reduce.6
  579.0 153.0 all-reduce.8
where the time goes:
time: 746 us; the launch traced here: 742 us
  waiting for transfers between devices  556 us (75%)
  other arithmetic  139 us (19%)
  matrix products  22.4 us (3%)
  between operations  14 us (2%)
    all_gather x2, waiting for transfers between devices, carried_in(): everything = lax.all_gather(x, axis)  267 us
    psum x1, waiting for transfers between devices, per_device(): down_total, up_total = lax.psum((grad_down, grad_up), 'seq')  154 us
    select_n x128, other arithmetic, step(): return jnp.where(reached, new, before)  133 us
    psum x1, waiting for transfers between devices, per_device(): inner_sum = lax.psum(partial_inner, 'mp') / math.sqrt(D)  69.7 us
    psum x1, waiting for transfers between devices, per_device(): inner_grad = lax.psum(partial_grad, 'mp') / math.sqrt(RANK)  66 us
  transfers between devices with their start and end apart: 5, of which 5 were waited for; matrix products, arithmetic and copies ran while one was open for 2% of the time, Pallas kernels for 0%

commit v1 on v0

v1 whole, which is shorter than its diff:
```python
import functools
import math

import jax
import jax.numpy as jnp
from jax import lax
from jax.experimental import pallas as pl
from jax.experimental.pallas import tpu as pltpu
from jax.sharding import PartitionSpec as P

D = 6144
HEAD = 128
RANK = 32
STEP = 250
CYCLE = 1000
TOK = 640
HEADS = 4
COLS = HEADS * HEAD
FEATS = 768
CHUNK = 128
CHUNKS = TOK // CHUNK
SIDE = 8
MESH = pl.DeviceIdType.MESH

friction = 0.2
peak_rate = 0.03
epsilon = 1e-06
step_rate = peak_rate * (math.cos(math.pi * ((STEP - 1) % CYCLE) / CYCLE) + 1.0)
spread = math.sqrt(2.0 * friction * step_rate)

F32 = jnp.float32
BF16 = jnp.bfloat16


def dot(a, b, ca, cb):
    return lax.dot_general(a, b, (((ca,), (cb,)), ((), ())), preferred_element_type=F32)


def feature_map(a):
    a = a.astype(F32)
    return jnp.where(a > 0.0, a + 1.0, jnp.exp(jnp.minimum(a, 0.0))).astype(BF16)


class Line:
    def __init__(self, me, device):
        self.me = me
        self.device = device

    def copy(self, src, dst, sems, send_at, recv_at, peer):
        return pltpu.make_async_remote_copy(
            src_ref=src,
            dst_ref=dst,
            send_sem=sems[0].at[send_at],
            recv_sem=sems[1].at[recv_at],
            device_id=self.device(peer),
            device_id_type=MESH,
        )

    def each(self, body):
        def run(i, carry):
            odd = i % 2
            k = SIDE // 2 + (i // 2) * (1 - 2 * odd) - odd
            body(lax.rem(self.me + k, SIDE))
            return carry

        lax.fori_loop(0, SIDE - 1, run, 0, unroll=True)

    def scatter(self, src, dst, sems):
        self.each(lambda t: self.copy(src.at[t], dst.at[self.me], sems, t, self.me, t).start())

    def spread(self, src, dst, sems):
        self.each(lambda t: self.copy(src, dst.at[self.me], sems, t, self.me, t).start())

    def wait_recv(self, dst, sems):
        self.each(lambda t: self.copy(dst.at[t], dst.at[t], sems, t, t, t).wait_recv())

    def wait_send(self, dst, sems):
        self.each(lambda t: self.copy(dst.at[t], dst.at[t], sems, t, t, t).wait_send())


class Scan:
    def __init__(self, zline, yline, bufs, sems, kind):
        self.z, self.y = zline, yline
        self.out, self.got, self.tot, self.back, self.result = bufs
        self.sz, self.sy, self.sb = sems[0:2], sems[2:4], sems[4:6]
        self.kind = kind

    def start(self):
        self.got[self.z.me] = self.out[self.z.me]
        self.z.scatter(self.out, self.got, self.sz)

    def start_part(self, low, high):
        for t in range(low, high):

            @pl.when(t == self.z.me)
            def _():
                self.got[t] = self.out[t]

            @pl.when(t != self.z.me)
            def _():
                at = self.z.me
                self.z.copy(self.out.at[t], self.got.at[at], self.sz, t, at, t).start()

    def middle(self):
        self.z.wait_recv(self.got, self.sz)
        if self.kind == "suffix":
            order = range(SIDE - 1, -1, -1)
        else:
            order = range(SIDE)
        total = None
        for at in order:
            if self.kind != "sum":
                self.back[at] = jnp.zeros_like(self.got[at]) if total is None else total
            total = self.got[at] if total is None else total + self.got[at]
        self.tot[self.y.me] = total
        self.y.spread(self.tot.at[self.y.me], self.tot, self.sy)

    def finish(self):
        self.y.wait_recv(self.tot, self.sy)
        base = jnp.zeros_like(self.tot[0])
        for at in range(SIDE):
            if self.kind == "sum":
                base = base + self.tot[at]
            else:
                counts = at < self.y.me if self.kind == "prefix" else at > self.y.me
                base = base + jnp.where(counts, self.tot[at], 0.0)
        if self.kind == "sum":
            self.result[self.z.me] = base
            self.z.spread(self.result.at[self.z.me], self.result, self.sb)
        else:
            for at in range(SIDE):
                self.back[at] = self.back[at] + base
            self.result[self.z.me] = self.back[self.z.me]
            self.z.scatter(self.back, self.result, self.sb)

    def wait(self):
        self.z.wait_recv(self.result, self.sb)

    def drain(self):
        self.z.wait_send(self.got, self.sz)
        self.y.wait_send(self.tot, self.sy)
        self.z.wait_send(self.result, self.sb)


class PairSum:
    def __init__(self, seq, mp, bufs, sems):
        self.seq = seq
        self.core, self.x = lax.rem(mp, 2), mp // 2
        self.part, self.other, self.row, self.total = bufs
        self.sem_a, self.sem_x, self.sem_b = sems

    def pair_copy(self, src, dst, sem):
        device = (self.seq, self.x * 2 + (1 - self.core))
        return pltpu.make_async_remote_copy(
            src_ref=src,
            dst_ref=dst,
            send_sem=sem.at[0],
            recv_sem=sem.at[1],
            device_id=device,
            device_id_type=MESH,
        )

    def x_copy(self, src, dst, send_at, recv_at, peer):
        return pltpu.make_async_remote_copy(
            src_ref=src,
            dst_ref=dst,
            send_sem=self.sem_x.at[send_at],
            recv_sem=self.sem_x.at[4 + recv_at],
            device_id=(self.seq, peer * 2 + self.core),
            device_id_type=MESH,
        )

    def peers(self):
        return [lax.rem(self.x + k, 4) for k in (2, 1, 3)]

    def start(self):
        self.first = self.pair_copy(self.part.at[1 - self.core], self.other, self.sem_a)
        self.first.start()

    def middle(self):
        self.first.wait_recv()
        self.row[self.x] = self.part[self.core] + self.other[...]
        mine = self.row.at[self.x]
        for t in self.peers():
            self.x_copy(mine, mine, t, self.x, t).start()

    def finish(self):
        for t in self.peers():
            self.x_copy(self.row.at[t], self.row.at[t], t, t, t).wait_recv()
        self.total[self.core] = (self.row[0] + self.row[1]) + (self.row[2] + self.row[3])
        mine = self.total.at[self.core]
        self.last = self.pair_copy(mine, mine, self.sem_b)
        self.last.start()

    def wait(self):
        other = self.total.at[1 - self.core]
        self.pair_copy(other, other, self.sem_b).wait_recv()
        return self.total[...].reshape(RANK, TOK)

    def drain(self):
        self.first.wait_send()
        for t in self.peers():
            self.x_copy(self.row.at[t], self.row.at[t], t, t, t).wait_send()
        self.last.wait_send()


def kernel(*refs):
    names = ("inputs", "queries", "keys", "values", "gain", "cot", "down", "up")
    names += ("mdown", "mup", "ndown", "nup")
    hbm = dict(zip(names, refs[:12]))
    scratch = list(refs[17:])

    def take(n):
        got = scratch[:n]
        del scratch[:n]
        return got

    x, q, k, v, gain, cot, down, up, mdown, mup, ndown, nup = take(12)
    vm = dict(zip(names, (x, q, k, v, gain, cot, down, up, mdown, mup, ndown, nup)))
    normed, o_down, o_mdown, o_up, o_mup = take(5)
    outs = list(zip((normed, o_down, o_mdown, o_up, o_mup), refs[12:17]))
    qf, kf, vmix, w, nearby, znear, grad, coef, low, near = take(10)
    kv_bufs, a_bufs, ub_bufs, gu_bufs, gd_bufs = take(5), take(5), take(5), take(5), take(5)
    p1_bufs, p2_bufs = take(4), take(4)
    load_sem, store_sem = take(2)

    def store(at):
        return pltpu.make_async_copy(*outs[at], store_sem.at[at])

    kv_sems, a_sems, ub_sems, gu_sems, gd_sems = take(6), take(6), take(6), take(6), take(6)
    p1_sems, p2_sems = take(3), take(3)

    seq, mp = lax.axis_index("seq"), lax.axis_index("mp")
    y, z = seq // SIDE, lax.rem(seq, SIDE)
    zline = Line(z, lambda t: (y * SIDE + t, mp))
    yline = Line(y, lambda t: (t * SIDE + z, mp))
    core, xpos = lax.rem(mp, 2), mp // 2

    kv = [
        Scan(zline, yline, [b.at[h] for b in kv_bufs], [m.at[h] for m in kv_sems], "prefix")
        for h in range(HEADS)
    ]
    pa = Scan(zline, yline, a_bufs, a_sems, "prefix")
    ub = Scan(zline, yline, ub_bufs, ub_sems, "suffix")
    gu = Scan(zline, yline, gu_bufs, gu_sems, "sum")
    gd = Scan(zline, yline, gd_bufs, gd_sems, "sum")
    p1 = PairSum(seq, mp, p1_bufs, p1_sems)
    p2 = PairSum(seq, mp, p2_bufs, p2_sems)

    barrier = pltpu.get_barrier_semaphore()
    signal = functools.partial(pl.semaphore_signal, barrier, inc=1, device_id_type=MESH)
    yline.each(lambda t: signal(device_id=yline.device(t)))
    zline.each(lambda t: signal(device_id=zline.device(t)))
    signal(device_id=(seq, xpos * 2 + (1 - core)))
    for t in p1.peers():
        signal(device_id=(seq, t * 2 + core))

    order = ("inputs", "down", "keys", "values", "queries", "up", "gain", "cot")
    order += ("mdown", "mup", "ndown", "nup")
    loads = {}
    for at, name in enumerate(order):
        loads[name] = pltpu.make_async_copy(hbm[name], vm[name], load_sem.at[at])
        loads[name].start()

    loads["inputs"].wait()
    loads["down"].wait()
    p1.part[...] = dot(down[...].astype(BF16), x[...], 1, 1).reshape(2, RANK // 2, TOK)

    def rows(i):
        return pl.ds(pl.multiple_of(i * CHUNK, CHUNK), CHUNK)

    def head(h):
        if isinstance(h, int):
            return slice(h * HEAD, (h + 1) * HEAD)
        return pl.ds(pl.multiple_of(h * HEAD, HEAD), HEAD)

    pl.semaphore_wait(barrier, 2 * (SIDE - 1) + 4)
    p1.start()

    loads["keys"].wait()

    def map_keys(i, c):
        kf[rows(i), :] = feature_map(k[rows(i), :])
        return c

    lax.fori_loop(0, CHUNKS, map_keys, 0)
    loads["values"].wait()

    def states(h):
        cols = slice(h * HEAD, (h + 1) * HEAD)
        kv_bufs[0][h] = dot(kf[:, cols], v[:, cols], 0, 0).reshape(SIDE, HEAD // SIDE, HEAD)
        kv[h].start()

    states(0)
    states(1)
    p1.middle()
    states(2)
    states(3)

    loads["queries"].wait()

    def map_queries(i, c):
        qf[rows(i), :] = feature_map(q[rows(i), :])
        return c

    lax.fori_loop(0, CHUNKS, map_queries, 0)

    def scores(h, c):
        for i in range(CHUNKS):
            at, width = i * CHUNK, (i + 1) * CHUNK
            s = dot(qf[at:width, head(h)], kf[:width, head(h)], 1, 1)
            t = lax.broadcasted_iota(jnp.int32, (CHUNK, width), 0) + at
            col = lax.broadcasted_iota(jnp.int32, (CHUNK, width), 1)
            w[h, at:width, :width] = jnp.where(t >= col, s, 0.0).astype(BF16)
        return c

    loads["up"].wait()
    p1.finish()
    kv[0].middle()
    kv[1].middle()
    inner = (p1.wait() * (1.0 / math.sqrt(D))).astype(BF16)
    coef[...] = inner
    share = dot(inner, kf[...], 1, 0)
    for h in range(HEADS):
        pa.out[2 * h : 2 * h + 2] = share[:, h * HEAD : (h + 1) * HEAD].reshape(2, RANK // 2, HEAD)
    pa.start()
    kv[2].middle()
    kv[3].middle()

    low[...] = jnp.transpose(inner.astype(F32)).astype(BF16)

    def mix(i, c):
        lifted = dot(low[rows(i), :], up[...].astype(BF16), 1, 0)
        vmix[rows(i), :] = (v[rows(i), :].astype(F32) + lifted * (1.0 / math.sqrt(RANK))).astype(BF16)
        return c

    lax.fori_loop(0, CHUNKS, mix, 0)
    lax.fori_loop(0, 1, scores, 0)
    pa.middle()
    kv[0].finish()
    kv[1].finish()
    lax.fori_loop(1, HEADS, scores, 0)

    def local(h, c):
        for i in range(CHUNKS):
            at, width = i * CHUNK, (i + 1) * CHUNK
            wc = w[h, at:width, :width]
            nearby[at:width, head(h)] = dot(wc, vmix[:width, head(h)], 1, 0)
            znear[h, at:width, :] = dot(wc, low[:width, :], 1, 0)
        return c

    kv[2].finish()
    kv[3].finish()
    pa.finish()
    lax.fori_loop(0, HEADS, local, 0)
    loads["gain"].wait()
    loads["cot"].wait()
    pa.wait()

    def attend(h, c):
        pre = pa.result[pl.ds(h * 2, 2)].reshape(RANK, HEAD).astype(BF16)
        uph = up[:, head(h)].astype(BF16)
        kv[h].wait()
        state = kv_bufs[4][h].reshape(HEAD, HEAD)
        state = (state + dot(pre, uph, 0, 0) * (1.0 / math.sqrt(RANK))).astype(BF16)
        g = gain[:, head(h)]
        for i in range(CHUNKS):
            r = slice(i * CHUNK, (i + 1) * CHUNK)
            summed = nearby[r, head(h)] + dot(qf[r, head(h)], state, 1, 0)
            gg = g * cot[r, head(h)].astype(F32)
            square = jnp.mean(summed * summed, axis=-1, keepdims=True)
            cross = jnp.mean(gg * summed, axis=-1, keepdims=True)
            inv = lax.rsqrt(square + epsilon)
            unit = summed * inv
            grad[r, head(h)] = (inv * gg - unit * (inv * inv * cross)).astype(BF16)
            normed[r, head(h)] = (g * unit).astype(BF16)
        return c

    def contract(h, c):
        uph = up[:, head(h)].astype(BF16)
        g = dot(uph, grad[:, head(h)], 1, 1).astype(BF16)
        p2_g[h] = g
        ub.out[pl.ds(h * 2, 2)] = dot(g, qf[:, head(h)], 1, 0).reshape(2, RANK // 2, HEAD)
        return c

    p2_g = scratch.pop(0)

    for h in range(HEADS):
        attend(h, 0)
    for h in range(HEADS):
        contract(h, 0)
        ub.start_part(2 * h, 2 * h + 2)
    store(0).start()
    def grad_up(h, c):
        pre = pa.result[pl.ds(h * 2, 2)].reshape(RANK, HEAD).astype(BF16)
        zsum = (znear[h] + dot(qf[:, head(h)], pre, 1, 1)).astype(BF16)
        gu.out[pl.ds(h * 2, 2)] = dot(zsum, grad[:, head(h)], 0, 0).reshape(2, RANK // 2, HEAD)
        return c

    lax.fori_loop(0, HEADS, grad_up, 0)
    near[...] = jnp.zeros_like(near)

    def back_near(h, c):
        for i in range(CHUNKS):
            at, width = i * CHUNK, (i + 1) * CHUNK
            near[:, at:width] += dot(p2_g[h, :, at:], w[h, at:, at:width], 1, 0)
        return c

    ub.middle()
    gu.start()
    lax.fori_loop(0, HEADS, back_near, 0)
    ub.finish()
    gu.middle()
    ub.wait()
    far = near[...]
    for h in range(HEADS):
        u = ub.result[2 * h : 2 * h + 2].reshape(RANK, HEAD).astype(BF16)
        far = far + dot(u, kf[:, h * HEAD : (h + 1) * HEAD], 1, 1)
    p2.part[...] = far.reshape(2, RANK // 2, TOK)
    p2.start()
    gu.finish()

    p2.middle()
    for name in ("mdown", "mup", "ndown", "nup"):
        loads[name].wait()
    p2.finish()
    gu.wait()
    up_total = gu.result[...].reshape(HEADS * RANK, HEAD)
    for h in range(HEADS):
        cols = slice(h * HEAD, (h + 1) * HEAD)
        total = up_total[h * RANK : (h + 1) * RANK] * (1.0 / math.sqrt(RANK))
        new = (1.0 - friction) * mup[:, cols] - step_rate * total + spread * nup[:, cols]
        o_mup[:, cols] = new
        o_up[:, cols] = up[:, cols] + new
    store(3).start()
    store(4).start()
    inner_grad = (p2.wait() * (1.0 / math.sqrt(RANK))).astype(BF16)
    share_down = dot(inner_grad, x[...], 1, 0) * (1.0 / math.sqrt(D))
    stacked = jnp.concatenate(
        [share_down[:, i * HEAD : (i + 1) * HEAD] for i in range(FEATS // HEAD)], axis=0
    )
    gd.out[...] = stacked.reshape(SIDE, RANK * FEATS // HEAD // SIDE, HEAD)
    gd.start()
    for h in range(HEADS):
        kv[h].drain()
    pa.drain()
    ub.drain()
    gd.middle()
    gu.drain()
    p1.drain()
    p2.drain()
    gd.finish()
    gd.wait()
    down_total = gd.result[...].reshape(RANK * FEATS // HEAD, HEAD)
    for i in range(FEATS // HEAD):
        cols = slice(i * HEAD, (i + 1) * HEAD)
        total = down_total[i * RANK : (i + 1) * RANK]
        new = (1.0 - friction) * mdown[:, cols] - step_rate * total + spread * ndown[:, cols]
        o_mdown[:, cols] = new
        o_down[:, cols] = down[:, cols] + new
    store(1).start()
    store(2).start()
    gd.drain()
    for at in range(len(outs)):
        store(at).wait()


def write_out(*refs):
    n = len(refs) // 2
    copies = [pltpu.make_async_copy(refs[i], refs[n + i], refs[-1].at[i]) for i in range(n)]
    for copy in copies:
        copy.start()
    for copy in copies:
        copy.wait()


def per_device(
    inputs,
    queries,
    key_rows,
    values,
    norm_gain,
    cotangent,
    adapter_down,
    adapter_up,
    moment_down,
    moment_up,
    noise_down,
    noise_up,
):
    args = (
        inputs,
        queries,
        key_rows,
        values,
        norm_gain.reshape(1, COLS),
        cotangent,
        adapter_down,
        adapter_up,
        moment_down,
        moment_up,
        noise_down,
        noise_up,
    )
    out_shape = (
        jax.ShapeDtypeStruct((TOK, COLS), BF16),
        jax.ShapeDtypeStruct((RANK, FEATS), F32),
        jax.ShapeDtypeStruct((RANK, FEATS), F32),
        jax.ShapeDtypeStruct((RANK, COLS), F32),
        jax.ShapeDtypeStruct((RANK, COLS), F32),
    )

    def scan_bufs(n):
        whole = pltpu.VMEM((SIDE, n, HEAD), F32)
        return [whole] * 5

    scratch = [pltpu.VMEM(a.shape, a.dtype) for a in args]
    scratch += [pltpu.VMEM(s.shape, s.dtype) for s in out_shape]
    scratch += [
        pltpu.VMEM((TOK, COLS), BF16),
        pltpu.VMEM((TOK, COLS), BF16),
        pltpu.VMEM((TOK, COLS), BF16),
        pltpu.VMEM((HEADS, TOK, TOK), BF16),
        pltpu.VMEM((TOK, COLS), F32),
        pltpu.VMEM((HEADS, TOK, RANK), F32),
        pltpu.VMEM((TOK, COLS), BF16),
        pltpu.VMEM((RANK, TOK), BF16),
        pltpu.VMEM((TOK, RANK), BF16),
        pltpu.VMEM((RANK, TOK), F32),
    ]
    scratch += [pltpu.VMEM((HEADS, SIDE, HEAD // SIDE, HEAD), F32)] * 5
    for n in (16, 16, 16, 24):
        scratch += scan_bufs(n)
    half = RANK // 2
    for _ in range(2):
        scratch += [
            pltpu.VMEM((2, half, TOK), F32),
            pltpu.VMEM((half, TOK), F32),
            pltpu.VMEM((4, half, TOK), F32),
            pltpu.VMEM((2, half, TOK), F32),
        ]
    sem = pltpu.SemaphoreType.DMA
    scratch += [sem((12,)), sem((5,))]
    scratch += [sem((HEADS, SIDE))] * 6
    scratch += [sem((SIDE,))] * 24
    scratch += [sem((2,)), sem((8,)), sem((2,))] * 2
    scratch += [pltpu.VMEM((HEADS, RANK, TOK), BF16)]
    anywhere = pl.BlockSpec(memory_space=pl.ANY)
    results = pl.pallas_call(
        kernel,
        out_shape=out_shape,
        in_specs=[anywhere] * len(args),
        out_specs=(anywhere,) * len(out_shape),
        scratch_shapes=scratch,
        compiler_params=pltpu.CompilerParams(
            collective_id=0, has_side_effects=True, vmem_limit_bytes=60 * 2**20
        ),
        name="fused_update",
    )(*args)
    return pl.pallas_call(
        write_out,
        out_shape=out_shape,
        in_specs=[pl.BlockSpec(memory_space=pltpu.VMEM)] * len(out_shape),
        out_specs=(anywhere,) * len(out_shape),
        scratch_shapes=[sem((len(out_shape),))],
        compiler_params=pltpu.CompilerParams(vmem_limit_bytes=60 * 2**20),
        name="write_out",
    )(*results)


def solution(mesh):
    return jax.shard_map(
        per_device,
        mesh=mesh,
        in_specs=(
            P("seq", "mp"),
            P("seq", "mp"),
            P("seq", "mp"),
            P("seq", "mp"),
            P("mp"),
            P("seq", "mp"),
            P(None, "mp"),
            P(None, "mp"),
            P(None, "mp"),
            P(None, "mp"),
            P(None, "mp"),
            P(None, "mp"),
        ),
        out_specs=(P("seq", "mp"), P(None, "mp"), P(None, "mp"), P(None, "mp"), P(None, "mp")),
        check_vma=False,
    )
```

time: 746 us -> 81.2 us (0.11)
  the two profiles are of different devices: /device:TPU:2 before, /device:TPU:8 now
where the time goes in v1:
time: 81.2 us; the launch traced here: 81 us
  Pallas kernels  80.4 us (99%)
    pallas_call x1, Pallas kernels, per_device(): pl.pallas_call(kernel, out_shape=out_shape, in_specs=[anywhere] * len(arg...  78.2 us
    pallas_call x1, Pallas kernels, per_device(): pl.pallas_call(write_out, out_shape=out_shape, in_specs=[pl.BlockSpec(mem...  2.17 us

profile of v1, /device:TPU:8, one launch (start us, length us, event | category | flops | bytes accessed | tf_op | source)
XLA Modules:
  0.0 81.0 jit_solution(2749874497501622504)
XLA Ops:
  0.6 78.2 %fused_update.1 = (bf16[640,512]{1,0:T(8,128)(2,1)}, f32[32,768]{1,0:T(8,128)}, f32[32,768]{1,0:T(8,128)}, f32[32,512]{1,0:T(8,128)}, f32[32,512]{1,0:T(8,128)}) custom-call(bf16[640,768]{1,0:T(8,128)(2,1)} %refs_0_.1, bf16[640,512]{1,0:T(8,128)(2,1)} %refs_1_.1, bf16[640,512]{1,0:T(8,128)(2,1)} %refs_2_.1, bf16[640,512]{1,0:T(8,128)(2,1)} %refs_3_.1, ...), custom_call_target="tpu_custom_call" | custom-call | tf_op jit(solution)/shard_map/fused_update/pallas_call | solution.py:549
  78.9 2.2 %write_out.1 = (bf16[640,512]{1,0:T(8,128)(2,1)}, f32[32,768]{1,0:T(8,128)}, f32[32,768]{1,0:T(8,128)}, f32[32,512]{1,0:T(8,128)}, f32[32,512]{1,0:T(8,128)}) custom-call(bf16[640,512]{1,0:T(8,128)(2,1)} %get-tuple-element.10.refs_0_, f32[32,768]{1,0:T(8,128)} %get-tuple-element.11.refs_1_, f32[32,768]{1,0:T(8,128)} %get-tuple-element.12.refs_2_, ...), custom_call_target="tpu_custom_call" | custom-call | tf_op jit(solution)/shard_map/write_out/pallas_call | solution.py:560

commit v2 on v1

--- a/solution.py
+++ b/solution.py
@@ -255,16 +255,28 @@
     for t in p1.peers():
         signal(device_id=(seq, t * 2 + core))
 
-    order = ("inputs", "down", "keys", "values", "queries", "up", "gain", "cot")
+    order = ("down", "inputs", "keys", "values", "queries", "up", "gain", "cot")
     order += ("mdown", "mup", "ndown", "nup")
     loads = {}
+    pieces = []
     for at, name in enumerate(order):
+        if name == "inputs":
+            for i in range(CHUNKS):
+                part = pl.ds(i * CHUNK, CHUNK)
+                piece = hbm[name].at[part], vm[name].at[part]
+                pieces.append(pltpu.make_async_copy(*piece, load_sem.at[12 + i]))
+                pieces[i].start()
+            continue
         loads[name] = pltpu.make_async_copy(hbm[name], vm[name], load_sem.at[at])
         loads[name].start()
 
-    loads["inputs"].wait()
     loads["down"].wait()
-    p1.part[...] = dot(down[...].astype(BF16), x[...], 1, 1).reshape(2, RANK // 2, TOK)
+    low_down = down[...].astype(BF16)
+    for i in range(CHUNKS):
+        pieces[i].wait()
+        cols = slice(i * CHUNK, (i + 1) * CHUNK)
+        share = dot(low_down, x[cols, :], 1, 1)
+        p1.part[:, :, cols] = share.reshape(2, RANK // 2, CHUNK)
 
     def rows(i):
         return pl.ds(pl.multiple_of(i * CHUNK, CHUNK), CHUNK)
@@ -284,6 +296,7 @@
         return c
 
     lax.fori_loop(0, CHUNKS, map_keys, 0)
+    p1.middle()
     loads["values"].wait()
 
     def states(h):
@@ -293,7 +306,6 @@
 
     states(0)
     states(1)
-    p1.middle()
     states(2)
     states(3)
 
@@ -314,6 +326,7 @@
             w[h, at:width, :width] = jnp.where(t >= col, s, 0.0).astype(BF16)
         return c
 
+    lax.fori_loop(0, 1, scores, 0)
     loads["up"].wait()
     p1.finish()
     kv[0].middle()
@@ -335,10 +348,11 @@
         return c
 
     lax.fori_loop(0, CHUNKS, mix, 0)
-    lax.fori_loop(0, 1, scores, 0)
-    pa.middle()
     kv[0].finish()
     kv[1].finish()
+    pa.middle()
+    kv[2].finish()
+    kv[3].finish()
     lax.fori_loop(1, HEADS, scores, 0)
 
     def local(h, c):
@@ -349,8 +363,6 @@
             znear[h, at:width, :] = dot(wc, low[:width, :], 1, 0)
         return c
 
-    kv[2].finish()
-    kv[3].finish()
     pa.finish()
     lax.fori_loop(0, HEADS, local, 0)
     loads["gain"].wait()
@@ -389,7 +401,7 @@
         attend(h, 0)
     for h in range(HEADS):
         contract(h, 0)
-        ub.start_part(2 * h, 2 * h + 2)
+    ub.start()
     store(0).start()
     def grad_up(h, c):
         pre = pa.result[pl.ds(h * 2, 2)].reshape(RANK, HEAD).astype(BF16)
@@ -411,6 +423,10 @@
     lax.fori_loop(0, HEADS, back_near, 0)
     ub.finish()
     gu.middle()
+    for h in range(HEADS):
+        kv[h].drain()
+    pa.drain()
+    p1.drain()
     ub.wait()
     far = near[...]
     for h in range(HEADS):
@@ -421,9 +437,17 @@
     gu.finish()
 
     p2.middle()
+    ub.drain()
     for name in ("mdown", "mup", "ndown", "nup"):
         loads[name].wait()
     p2.finish()
+    inner_grad = (p2.wait() * (1.0 / math.sqrt(RANK))).astype(BF16)
+    share_down = dot(inner_grad, x[...], 1, 0) * (1.0 / math.sqrt(D))
+    stacked = jnp.concatenate(
+        [share_down[:, i * HEAD : (i + 1) * HEAD] for i in range(FEATS // HEAD)], axis=0
+    )
+    gd.out[...] = stacked.reshape(SIDE, RANK * FEATS // HEAD // SIDE, HEAD)
+    gd.start()
     gu.wait()
     up_total = gu.result[...].reshape(HEADS * RANK, HEAD)
     for h in range(HEADS):
@@ -434,20 +458,8 @@
         o_up[:, cols] = up[:, cols] + new
     store(3).start()
     store(4).start()
-    inner_grad = (p2.wait() * (1.0 / math.sqrt(RANK))).astype(BF16)
-    share_down = dot(inner_grad, x[...], 1, 0) * (1.0 / math.sqrt(D))
-    stacked = jnp.concatenate(
-        [share_down[:, i * HEAD : (i + 1) * HEAD] for i in range(FEATS // HEAD)], axis=0
-    )
-    gd.out[...] = stacked.reshape(SIDE, RANK * FEATS // HEAD // SIDE, HEAD)
-    gd.start()
-    for h in range(HEADS):
-        kv[h].drain()
-    pa.drain()
-    ub.drain()
     gd.middle()
     gu.drain()
-    p1.drain()
     p2.drain()
     gd.finish()
     gd.wait()
@@ -466,11 +478,24 @@
 
 
 def write_out(*refs):
-    n = len(refs) // 2
-    copies = [pltpu.make_async_copy(refs[i], refs[n + i], refs[-1].at[i]) for i in range(n)]
-    for copy in copies:
+    n = len(refs) // 3
+    pieces = []
+    for at in range(n):
+        src, dst, held = refs[at], refs[n + at], refs[2 * n + at]
+        steps = 4 if at == 0 else 1
+        rows = src.shape[0] // steps
+        for k in range(steps):
+            part = pl.ds(k * rows, rows)
+            pieces.append((src.at[part], held.at[part], dst.at[part]))
+    sem = refs[-1]
+    reads = [pltpu.make_async_copy(p[0], p[1], sem.at[0, i]) for i, p in enumerate(pieces)]
+    writes = [pltpu.make_async_copy(p[1], p[2], sem.at[1, i]) for i, p in enumerate(pieces)]
+    for copy in reads:
         copy.start()
-    for copy in copies:
+    for read, write in zip(reads, writes):
+        read.wait()
+        write.start()
+    for copy in writes:
         copy.wait()
 
 
@@ -540,7 +565,7 @@
             pltpu.VMEM((2, half, TOK), F32),
         ]
     sem = pltpu.SemaphoreType.DMA
-    scratch += [sem((12,)), sem((5,))]
+    scratch += [sem((12 + CHUNKS,)), sem((5,))]
     scratch += [sem((HEADS, SIDE))] * 6
     scratch += [sem((SIDE,))] * 24
     scratch += [sem((2,)), sem((8,)), sem((2,))] * 2
@@ -560,9 +585,9 @@
     return pl.pallas_call(
         write_out,
         out_shape=out_shape,
-        in_specs=[pl.BlockSpec(memory_space=pltpu.VMEM)] * len(out_shape),
+        in_specs=[anywhere] * len(out_shape),
         out_specs=(anywhere,) * len(out_shape),
-        scratch_shapes=[sem((len(out_shape),))],
+        scratch_shapes=[pltpu.VMEM(s.shape, s.dtype) for s in out_shape] + [sem((2, 8))],
         compiler_params=pltpu.CompilerParams(vmem_limit_bytes=60 * 2**20),
         name="write_out",
     )(*results)

time: 81.2 us -> 80.7 us (level)
  no operation moved by 1% of the time
where the time goes in v2:
time: 80.7 us; the launch traced here: 80.5 us
  Pallas kernels  79.9 us (99%)
    pallas_call x1, Pallas kernels, per_device(): pl.pallas_call(kernel, out_shape=out_shape, in_specs=[anywhere] * len(arg...  77.8 us
    pallas_call x1, Pallas kernels, per_device(): pl.pallas_call(write_out, out_shape=out_shape, in_specs=[anywhere] * len(...  2.07 us

profile of v2, /device:TPU:8, one launch (start us, length us, event | category | flops | bytes accessed | tf_op | source)
XLA Modules:
  0.0 80.5 jit_solution(3060070723781246295)
XLA Ops:
  0.6 77.8 %fused_update.1 = (bf16[640,512]{1,0:T(8,128)(2,1)}, f32[32,768]{1,0:T(8,128)}, f32[32,768]{1,0:T(8,128)}, f32[32,512]{1,0:T(8,128)}, f32[32,512]{1,0:T(8,128)}) custom-call(bf16[640,768]{1,0:T(8,128)(2,1)} %refs_0_.1, bf16[640,512]{1,0:T(8,128)(2,1)} %refs_1_.1, bf16[640,512]{1,0:T(8,128)(2,1)} %refs_2_.1, bf16[640,512]{1,0:T(8,128)(2,1)} %refs_3_.1, ...), custom_call_target="tpu_custom_call" | custom-call | tf_op jit(solution)/shard_map/fused_update/pallas_call | solution.py:574
  78.5 2.1 %write_out.1 = (bf16[640,512]{1,0:T(8,128)(2,1)}, f32[32,768]{1,0:T(8,128)}, f32[32,768]{1,0:T(8,128)}, f32[32,512]{1,0:T(8,128)}, f32[32,512]{1,0:T(8,128)}) custom-call(bf16[640,512]{1,0:T(8,128)(2,1)} %get-tuple-element.10.refs_0_, f32[32,768]{1,0:T(8,128)} %get-tuple-element.11.refs_1_, f32[32,768]{1,0:T(8,128)} %get-tuple-element.12.refs_2_, ...), custom_call_target="tpu_custom_call" | custom-call | tf_op jit(solution)/shard_map/write_out/pallas_call | solution.py:585

commit v3 on v2

--- a/solution.py
+++ b/solution.py
@@ -326,17 +326,16 @@
             w[h, at:width, :width] = jnp.where(t >= col, s, 0.0).astype(BF16)
         return c
 
-    lax.fori_loop(0, 1, scores, 0)
     loads["up"].wait()
     p1.finish()
     kv[0].middle()
-    kv[1].middle()
     inner = (p1.wait() * (1.0 / math.sqrt(D))).astype(BF16)
     coef[...] = inner
     share = dot(inner, kf[...], 1, 0)
     for h in range(HEADS):
         pa.out[2 * h : 2 * h + 2] = share[:, h * HEAD : (h + 1) * HEAD].reshape(2, RANK // 2, HEAD)
     pa.start()
+    kv[1].middle()
     kv[2].middle()
     kv[3].middle()
 
@@ -353,7 +352,7 @@
     pa.middle()
     kv[2].finish()
     kv[3].finish()
-    lax.fori_loop(1, HEADS, scores, 0)
+    lax.fori_loop(0, HEADS, scores, 0)
 
     def local(h, c):
         for i in range(CHUNKS):
@@ -434,9 +433,8 @@
         far = far + dot(u, kf[:, h * HEAD : (h + 1) * HEAD], 1, 1)
     p2.part[...] = far.reshape(2, RANK // 2, TOK)
     p2.start()
+    p2.middle()
     gu.finish()
-
-    p2.middle()
     ub.drain()
     for name in ("mdown", "mup", "ndown", "nup"):
         loads[name].wait()

time: 80.7 us -> 80 us (level)
  no operation moved by 1% of the time
where the time goes in v3:
time: 80 us; the launch traced here: 79.9 us
  Pallas kernels  79.2 us (99%)
    pallas_call x1, Pallas kernels, per_device(): pl.pallas_call(kernel, out_shape=out_shape, in_specs=[anywhere] * len(arg...  77.1 us
    pallas_call x1, Pallas kernels, per_device(): pl.pallas_call(write_out, out_shape=out_shape, in_specs=[anywhere] * len(...  2.07 us

profile of v3, /device:TPU:8, one launch (start us, length us, event | category | flops | bytes accessed | tf_op | source)
XLA Modules:
  0.0 79.9 jit_solution(9987485341851377385)
XLA Ops:
  0.6 77.1 %fused_update.1 = (bf16[640,512]{1,0:T(8,128)(2,1)}, f32[32,768]{1,0:T(8,128)}, f32[32,768]{1,0:T(8,128)}, f32[32,512]{1,0:T(8,128)}, f32[32,512]{1,0:T(8,128)}) custom-call(bf16[640,768]{1,0:T(8,128)(2,1)} %refs_0_.1, bf16[640,512]{1,0:T(8,128)(2,1)} %refs_1_.1, bf16[640,512]{1,0:T(8,128)(2,1)} %refs_2_.1, bf16[640,512]{1,0:T(8,128)(2,1)} %refs_3_.1, ...), custom_call_target="tpu_custom_call" | custom-call | tf_op jit(solution)/shard_map/fused_update/pallas_call | solution.py:572
  77.8 2.1 %write_out.1 = (bf16[640,512]{1,0:T(8,128)(2,1)}, f32[32,768]{1,0:T(8,128)}, f32[32,768]{1,0:T(8,128)}, f32[32,512]{1,0:T(8,128)}, f32[32,512]{1,0:T(8,128)}) custom-call(bf16[640,512]{1,0:T(8,128)(2,1)} %get-tuple-element.10.refs_0_, f32[32,768]{1,0:T(8,128)} %get-tuple-element.11.refs_1_, f32[32,768]{1,0:T(8,128)} %get-tuple-element.12.refs_2_, ...), custom_call_target="tpu_custom_call" | custom-call | tf_op jit(solution)/shard_map/write_out/pallas_call | solution.py:583
